TPU v7x, 32 devices: a whole 2x2x4 slice. The times are simulated.
32 devices in a mesh: gene: 4 (over y, core), rows: 8 (over z, x).
Axes of the slice: x: 2, y: 2, z: 4, core: 2. Of those that a mesh axis runs over, the one named last changes fastest.
Arguments:
- density: float32 [128, 256, 1024], P('gene', 'rows'), may hold values from 0.05 to 1, as said below
- effect_first: float32 [7], replicated, may hold values from 0.02 to 0.04
- effect_second: float32 [7], replicated, may hold values from 0 to 0.025
- decay_pair: float32 [2], replicated, may hold values from 0.08 to 0.5, as said below
- switch_rates: float32 [2, 7], replicated, may hold values from 0.1 to 3
- gene_place: int32 [7], replicated, may hold values from 0 to 6, each once
- bound_first: int32 [128], P('gene'), may hold values from 128 to 256
- bound_second: int32 [128], P('gene'), may hold values from 512 to 1024
Outputs:
- evolved: float32 [128, 256, 1024], P('gene', 'rows')
Inputs may be any that keep to these rules, and one draw needn't show every extreme that they name: `gene_place`: a permutation: each bit 0 to 6 holds exactly one gene. `density`: positive probabilities. decay_pair[0] lies in 0.42 to 0.5 and decay_pair[1] in 0.08 to 0.22.
All inputs are finite; a program needn't handle non-finite values.
Results may differ from a plain program's by a relative error of at most 0.0003.
Values sent between devices are 32-bit elements; how exact they have to be, the bound alone decides.
A program may use at most 128 MiB of HBM per device.

v0:
```python
import functools

import jax
import jax.numpy as jnp
from jax import lax
from jax.experimental import pallas as pl
from jax.experimental.pallas import tpu as pltpu
from jax.sharding import PartitionSpec as P

GENES = 7
SUB = 4
TILE = 8
LANES = 128
EARLY = 10
MESH = pl.DeviceIdType.MESH


def kernel(
    count, rows, width, peers, total_rows,
    density_ref, effect_one, effect_two, decay_ref, rates_ref, place_ref, bound_one, bound_two,
    result_ref,
    x_ref, out_ref, birth_ref, bound_ref, limit_ref, grow_ref, curve_ref, fall_ref, factor_ref,
    main, edge, late, late_edge, *rest,
):
    stages = len(rest) - 8
    arrived = rest[:stages]
    (send_sem, recv_sem, halo_send, halo_recv, late_send, late_recv, in_sem,
     out_sem) = rest[stages:]
    tiles = count // TILE
    local_bits = count.bit_length() - 1
    gene = lax.axis_index("gene")
    place = lax.axis_index("rows")
    first = place * rows
    partners = [gene + (1 << q) - 2 * (gene & (1 << q)) for q in range(stages)]
    has_prev, has_next = place > 0, place < peers - 1

    barrier = pltpu.get_barrier_semaphore()
    for partner in partners:
        pl.semaphore_signal(barrier, inc=1, device_id=(partner, place), device_id_type=MESH)

    @pl.when(has_prev)
    def _():
        pl.semaphore_signal(barrier, inc=1, device_id=(gene, place - 1), device_id_type=MESH)

    @pl.when(has_next)
    def _():
        pl.semaphore_signal(barrier, inc=1, device_id=(gene, place + 1), device_id_type=MESH)

    def fetch(block):
        piece = pl.ds(TILE * block, TILE)
        return pltpu.make_async_copy(
            density_ref.at[:, piece, :], x_ref.at[:, piece, :], in_sem.at[block])

    def deliver(block):
        piece = pl.ds(TILE * block, TILE)
        return pltpu.make_async_copy(
            out_ref.at[:, piece, :], result_ref.at[:, piece, :], out_sem.at[block])

    blocks_in = rows // TILE
    fetch_order = [0, blocks_in - 1] + list(range(1, blocks_in - 1))
    for block in fetch_order:
        fetch(block).start()

    def loop(low, high, step):
        def run(i, carry):
            step(i)
            return carry
        lax.fori_loop(low, high, run, 0)

    def part(i):
        return pl.ds(TILE * i, TILE)

    def wide(value):
        return jnp.concatenate([value] * (width // LANES), axis=1)

    def by_bit(values, bit):
        total = jnp.float32(0.0)
        for g in range(GENES):
            total = total + jnp.where(place_ref[g] == bit, values(g), 0.0)
        return total

    def spread(s):
        line = pl.ds(s, 1)
        bound_ref[line, :] = jnp.full((1, LANES), bound_one[s].astype(jnp.float32))
        limit_ref[line, :] = jnp.full((1, LANES), bound_two[s].astype(jnp.float32))

    def prepare():
        loop(0, count, spread)
        cols = lax.broadcasted_iota(jnp.int32, (TILE, width), 1).astype(jnp.float32)
        curve_ref[...] = width / (width + 3.0 * cols)
        fall_ref[...] = decay_ref[1] * cols * (1.0 / width)
        first_effects = [by_bit(lambda g: effect_one[g], bit) for bit in range(GENES)]
        second_effects = [by_bit(lambda g: effect_two[g], bit) for bit in range(GENES)]
        line = lax.broadcasted_iota(jnp.int32, (TILE, LANES), 0)
        for i in range(tiles):
            state = gene * count + TILE * i + line
            one = jnp.full((TILE, LANES), 0.02, jnp.float32)
            two = jnp.full((TILE, LANES), 0.02, jnp.float32)
            for bit in range(GENES):
                held = ((state >> bit) & 1).astype(jnp.float32)
                one = one + held * first_effects[bit]
                two = two + held * second_effects[bit]
            birth_ref[part(i), :] = one
            grow_ref[part(i), :] = jnp.where(
                cols + 1.0 < wide(limit_ref[part(i), :]), wide(two), 0.0)
        for bit in range(GENES):
            rate_on = jnp.full((TILE, LANES), by_bit(lambda g: rates_ref[0, g], bit))
            rate_off = jnp.full((TILE, LANES), by_bit(lambda g: rates_ref[1, g], bit))
            total = rate_on + rate_off
            fading = jnp.exp(-total)
            factor_ref[bit] = (rate_off + rate_on * fading) / total
            factor_ref[GENES + bit] = rate_off * (1.0 - fading) / total
            factor_ref[2 * GENES + bit] = rate_on * (1.0 - fading) / total
            factor_ref[3 * GENES + bit] = (rate_on + rate_off * fading) / total

    def load(row):
        return x_ref[:, row, :]

    def update(buf, slot, row, out=False):
        level = (first + row).astype(jnp.float32)
        side = (total_rows + 3.0 * level) * (1.0 / (4.0 * total_rows))
        drop = decay_ref[0] * level * (1.0 / total_rows)
        drop_next = decay_ref[0] * (level + 1.0) * (1.0 / total_rows)
        fall, curve = fall_ref[...], curve_ref[...]
        stay = (1.0 - drop) - fall
        values = []
        for i in range(tiles):
            above = buf[slot, part(i), :]
            here = buf[slot + 1, part(i), :]
            below = buf[slot + 2, part(i), :]
            birth, bound = birth_ref[part(i), :], bound_ref[part(i), :]
            rise = wide(jnp.where(level + 1.0 < bound, birth, 0.0))
            rise_above = wide(jnp.where(level < bound, birth, 0.0))
            right = here * (grow_ref[part(i), :] * side)
            left = here * fall
            value = here * stay + drop_next * below
            value = value + curve * (rise_above * above - rise * here)
            value = value + (pltpu.roll(right, 1, 1) - right)
            values.append(value + pltpu.roll(left, width - 1, 1))
        for i, value in enumerate(values):
            if out:
                out_ref[part(i), row, :] = value
            else:
                buf[slot, part(i), :] = value

    def triangle(buf, slots, base, last):
        for t in range(1, last + 1):
            loop(0, slots - 2 * t, lambda j, t=t: update(buf, j, base + j + t))

    def wave(buf, k, out=False):
        for t in range(1, SUB + 1):
            slot = k - 2 * (t - 1)
            update(buf, slot, slot + t, out=out and t == SUB)

    def slot_of(row):
        return lax.rem(row + rows - SUB, rows)

    def mine(q, row):
        return main.at[slot_of(row)] if q == 0 else arrived[q - 1].at[row]

    def exchange(q, row):
        return pltpu.make_async_remote_copy(
            src_ref=mine(q, row), dst_ref=arrived[q].at[row],
            send_sem=send_sem.at[q, row], recv_sem=recv_sem.at[q, row],
            device_id=(partners[q], place), device_id_type=MESH)

    def factor(kind, bit):
        return factor_ref[kind * GENES + bit]

    def mix(q, row):
        bit = local_bits + q
        on = (gene >> q) & 1 == 1
        keep = wide(jnp.where(on, factor(3, bit), factor(0, bit)))
        take = wide(jnp.where(on, factor(2, bit), factor(1, bit)))
        own = mine(q, row)
        return [keep * own[part(i), :] + take * arrived[q][row, part(i), :] for i in range(tiles)]

    def advance(q, row):
        exchange(q, row).wait_recv()
        for i, value in enumerate(mix(q, row)):
            arrived[q][row, part(i), :] = value
        exchange(q + 1, row).start()

    def finish(row):
        q = stages - 1
        exchange(q, row).wait_recv()
        blocks = mix(q, row)
        index = lax.broadcasted_iota(jnp.int32, (TILE, LANES), 0)
        for bit in range(3):
            on = (index >> bit) & 1 == 1
            keep = wide(jnp.where(on, factor(3, bit), factor(0, bit)))
            take = wide(jnp.where(on, factor(2, bit), factor(1, bit)))
            swap = wide(on)
            gap = 1 << bit
            mixed = []
            for block in blocks:
                other = pltpu.roll(block, gap, 0)
                if 2 * gap != TILE:
                    other = jnp.where(swap, other, pltpu.roll(block, TILE - gap, 0))
                mixed.append(keep * block + take * other)
            blocks = mixed
        for bit in range(3, local_bits):
            gap = 1 << (bit - 3)
            mixed = list(blocks)
            for i in range(tiles):
                if not i & gap:
                    low, high = blocks[i], blocks[i + gap]
                    mixed[i] = wide(factor(0, bit)) * low + wide(factor(1, bit)) * high
                    mixed[i + gap] = wide(factor(2, bit)) * low + wide(factor(3, bit)) * high
            blocks = mixed
        for i in range(tiles):
            late[row, part(i), :] = blocks[i]

    def halo(grid, rim, sends, recvs):
        upward = pltpu.make_async_remote_copy(
            src_ref=grid.at[pl.ds(rows - SUB, SUB)], dst_ref=rim.at[pl.ds(0, SUB)],
            send_sem=sends.at[0], recv_sem=recvs.at[0],
            device_id=(gene, place + 1), device_id_type=MESH)
        downward = pltpu.make_async_remote_copy(
            src_ref=rim.at[pl.ds(SUB, SUB)], dst_ref=grid.at[pl.ds(rows, SUB)],
            send_sem=sends.at[1], recv_sem=recvs.at[1],
            device_id=(gene, place - 1), device_id_type=MESH)
        return upward, downward

    def halo_start(copies):
        @pl.when(has_next)
        def _():
            copies[0].start()

        @pl.when(has_prev)
        def _():
            copies[1].start()

    def halo_top(copies, rim):
        @pl.when(has_prev)
        def _():
            copies[1].wait_send()
            copies[0].wait_recv()

        @pl.when(jnp.logical_not(has_prev))
        def _():
            rim[pl.ds(0, SUB)] = jnp.zeros((SUB, count, width), jnp.float32)

    def halo_bottom(copies, grid):
        @pl.when(has_next)
        def _():
            copies[0].wait_send()
            copies[1].wait_recv()

        @pl.when(jnp.logical_not(has_next))
        def _():
            grid[pl.ds(rows, SUB)] = jnp.zeros((SUB, count, width), jnp.float32)

    def load_both(row):
        value = load(row)
        main[row] = value
        edge[SUB + row] = value

    def load_main(row):
        main[row] = load(row)

    prepare()
    for block in fetch_order[:2]:
        fetch(block).wait()
    loop(0, SUB, load_both)
    loop(rows - SUB, rows, load_main)
    met = stages + jnp.where(has_prev, 1, 0) + jnp.where(has_next, 1, 0)
    pl.semaphore_wait(barrier, met)

    early_halo = halo(main, edge, halo_send, halo_recv)
    halo_start(early_halo)
    loop(SUB, 2 * SUB, load_both)
    for block in fetch_order[2:]:
        fetch(block).wait()
    triangle(main, 2 * SUB, 0, SUB - 1)

    def produce(k):
        @pl.when(k + 2 < rows - SUB)
        def _():
            load_main(k + 2)
        wave(main, k)
        exchange(0, k - 2).start()

    def produce_and_pass(k):
        produce(k)
        advance(0, k - 3)

    early = SUB + EARLY
    produce(6)
    loop(7, early + 3, produce_and_pass)
    loop(early + 3, rows - SUB, produce)
    halo_bottom(early_halo, main)
    loop(rows - SUB, rows + 2, produce)
    halo_top(early_halo, edge)
    triangle(edge, 3 * SUB, -SUB, SUB)

    def give(row):
        main[rows - SUB + row] = edge[row]
        exchange(0, row).start()

    loop(0, SUB, give)
    order = [(SUB, early), (rows - SUB, rows), (0, SUB), (early, rows - SUB)]
    for low, high in order[1:]:
        loop(low, high, lambda row: advance(0, row))
    for q in range(1, stages - 1):
        for low, high in order:
            loop(low, high, lambda row, q=q: advance(q, row))

    for low, high in order[:-1]:
        loop(low, high, finish)

    def copy_edge(row):
        late_edge[SUB + row] = late[row]

    loop(0, 2 * SUB, copy_edge)
    late_halo = halo(late, late_edge, late_send, late_recv)
    halo_start(late_halo)

    def emit(k):
        wave(late, k, out=True)

    def finish_and_emit(k):
        finish(k + 2)
        emit(k)

    triangle(late, 2 * SUB, 0, SUB - 1)
    loop(6, early - 2, emit)
    loop(early - 2, rows - SUB - 6, finish_and_emit)
    deliver(1).start()
    halo_top(late_halo, late_edge)
    triangle(late_edge, 3 * SUB, -SUB, SUB - 1)
    loop(0, SUB, lambda j: update(late_edge, j, j, out=True))
    deliver(0).start()
    loop(rows - SUB - 6, rows - SUB - 2, finish_and_emit)
    deliver(2).start()
    halo_bottom(late_halo, late)
    loop(rows - SUB - 2, rows + 2, emit)
    deliver(3).start()
    for q in range(stages):
        loop(0, rows, lambda row, q=q: exchange(q, row).wait_send())
    for block in range(blocks_in):
        deliver(block).wait()


def body(peers, genes, density, *params):
    count, rows, width = density.shape
    stages = genes.bit_length() - 1
    row = (count, width)
    smem = pl.BlockSpec(memory_space=pltpu.SMEM)
    whole = pl.BlockSpec(memory_space=pl.ANY)

    def vmem(*shape):
        return pltpu.VMEM(shape, jnp.float32)

    return pl.pallas_call(
        functools.partial(kernel, count, rows, width, peers, float(rows * peers)),
        out_shape=jax.ShapeDtypeStruct(density.shape, jnp.float32),
        in_specs=[whole] + [smem] * len(params),
        out_specs=whole,
        scratch_shapes=[
            vmem(*density.shape),
            vmem(*density.shape),
            vmem(count, LANES),
            vmem(count, LANES),
            vmem(count, LANES),
            vmem(*row),
            vmem(TILE, width),
            vmem(TILE, width),
            vmem(4 * GENES, TILE, LANES),
            vmem(rows + SUB, *row),
            vmem(3 * SUB, *row),
            vmem(rows + SUB, *row),
            vmem(3 * SUB, *row),
        ] + [vmem(rows, *row)] * stages + [
            pltpu.SemaphoreType.DMA((stages, rows)),
            pltpu.SemaphoreType.DMA((stages, rows)),
            pltpu.SemaphoreType.DMA((2,)),
            pltpu.SemaphoreType.DMA((2,)),
            pltpu.SemaphoreType.DMA((2,)),
            pltpu.SemaphoreType.DMA((2,)),
            pltpu.SemaphoreType.DMA((rows // TILE,)),
            pltpu.SemaphoreType.DMA((rows // TILE,)),
        ],
        compiler_params=pltpu.CompilerParams(
            collective_id=0, has_side_effects=True, vmem_limit_bytes=60 * 1024 * 1024),
    )(density, *params)


def solution(mesh):
    placed = (P("gene", "rows", None), P(), P(), P(), P(), P(), P("gene"), P("gene"))
    return jax.shard_map(
        functools.partial(body, mesh.shape["rows"], mesh.shape["gene"]),
        mesh=mesh, in_specs=placed, out_specs=P("gene", "rows", None), check_vma=False,
    )
```

profile of v0, /device:TPU:8, one launch (start us, length us, event | category | flops | bytes accessed | tf_op | source)
XLA Modules:
  0.0 110.5 jit_solution(14135287716020700864)
XLA Ops:
  0.0 105.7 %shard_map.82 = f32[32,32,1024]{2,1,0:T(8,128)} custom-call(f32[32,32,1024]{2,1,0:T(8,128)} %density_ref.1, f32[7]{0:T(128)} %effect_one.1, f32[7]{0:T(128)} %effect_two.1, f32[2]{0:T(128)} %decay_ref.1, f32[2,7]{1,0:T(2,128)} %rates_ref.1, s32[7]{0:T(128)} %place_ref.1, s32[32]{0:T(128)} %bound_one.1, s32[32]{0:T(128)} %bound_two.1), custom_call_target="tpu_custom_call" | custom-call | tf_op jit(solution)/shard_map/pallas_call | solution.py:355
  105.7 4.8 %copy.10 = f32[32,32,1024]{2,1,0:T(8,128)} copy(f32[32,32,1024]{2,1,0:T(8,128)} %shard_map.82) | data formatting | bytes 8388608
where the time goes:
time: 112 us; the launch traced here: 111 us
  Pallas kernels  106 us (95%)
  local copies, waits for them, and re-layouts  4.79 us (4%)
    pallas_call x1, Pallas kernels, body(): pl.pallas_call(functools.partial(kernel, count, rows, width, peers, float...  106 us
    unnamed x1, local copies, waits for them, and re-layouts  4.79 us

commit v1 on v0

--- a/solution.py
+++ b/solution.py
@@ -2,6 +2,7 @@
 
 import jax
 import jax.numpy as jnp
+import numpy as np
 from jax import lax
 from jax.experimental import pallas as pl
 from jax.experimental.pallas import tpu as pltpu
@@ -17,15 +18,13 @@
 
 def kernel(
     count, rows, width, peers, total_rows,
-    density_ref, effect_one, effect_two, decay_ref, rates_ref, place_ref, bound_one, bound_two,
-    result_ref,
-    x_ref, out_ref, birth_ref, bound_ref, limit_ref, grow_ref, curve_ref, fall_ref, factor_ref,
+    density_ref, param_ref, out_ref,
+    x_ref, birth_ref, bound_ref, limit_ref, grow_ref, curve_ref, fall_ref, factor_ref,
     main, edge, late, late_edge, *rest,
 ):
-    stages = len(rest) - 8
+    stages = len(rest) - 7
     arrived = rest[:stages]
-    (send_sem, recv_sem, halo_send, halo_recv, late_send, late_recv, in_sem,
-     out_sem) = rest[stages:]
+    send_sem, recv_sem, halo_send, halo_recv, late_send, late_recv, in_sem = rest[stages:]
     tiles = count // TILE
     local_bits = count.bit_length() - 1
     gene = lax.axis_index("gene")
@@ -51,13 +50,7 @@
         return pltpu.make_async_copy(
             density_ref.at[:, piece, :], x_ref.at[:, piece, :], in_sem.at[block])
 
-    def deliver(block):
-        piece = pl.ds(TILE * block, TILE)
-        return pltpu.make_async_copy(
-            out_ref.at[:, piece, :], result_ref.at[:, piece, :], out_sem.at[block])
-
-    blocks_in = rows // TILE
-    fetch_order = [0, blocks_in - 1] + list(range(1, blocks_in - 1))
+    fetch_order = [0, 1] + list(range(2, rows // TILE))[::-1]
     for block in fetch_order:
         fetch(block).start()
 
@@ -73,24 +66,26 @@
     def wide(value):
         return jnp.concatenate([value] * (width // LANES), axis=1)
 
-    def by_bit(values, bit):
+    decays = [param_ref[5, 0], param_ref[5, 1]]
+
+    def by_bit(group, bit):
         total = jnp.float32(0.0)
         for g in range(GENES):
-            total = total + jnp.where(place_ref[g] == bit, values(g), 0.0)
+            total = total + jnp.where(param_ref[4, g] == float(bit), param_ref[group, g], 0.0)
         return total
 
     def spread(s):
         line = pl.ds(s, 1)
-        bound_ref[line, :] = jnp.full((1, LANES), bound_one[s].astype(jnp.float32))
-        limit_ref[line, :] = jnp.full((1, LANES), bound_two[s].astype(jnp.float32))
+        bound_ref[line, :] = jnp.full((1, LANES), param_ref[6, s])
+        limit_ref[line, :] = jnp.full((1, LANES), param_ref[7, s])
 
     def prepare():
         loop(0, count, spread)
         cols = lax.broadcasted_iota(jnp.int32, (TILE, width), 1).astype(jnp.float32)
         curve_ref[...] = width / (width + 3.0 * cols)
-        fall_ref[...] = decay_ref[1] * cols * (1.0 / width)
-        first_effects = [by_bit(lambda g: effect_one[g], bit) for bit in range(GENES)]
-        second_effects = [by_bit(lambda g: effect_two[g], bit) for bit in range(GENES)]
+        fall_ref[...] = decays[1] * cols * (1.0 / width)
+        first_effects = [by_bit(0, bit) for bit in range(GENES)]
+        second_effects = [by_bit(1, bit) for bit in range(GENES)]
         line = lax.broadcasted_iota(jnp.int32, (TILE, LANES), 0)
         for i in range(tiles):
             state = gene * count + TILE * i + line
@@ -104,8 +99,8 @@
             grow_ref[part(i), :] = jnp.where(
                 cols + 1.0 < wide(limit_ref[part(i), :]), wide(two), 0.0)
         for bit in range(GENES):
-            rate_on = jnp.full((TILE, LANES), by_bit(lambda g: rates_ref[0, g], bit))
-            rate_off = jnp.full((TILE, LANES), by_bit(lambda g: rates_ref[1, g], bit))
+            rate_on = jnp.full((TILE, LANES), by_bit(2, bit))
+            rate_off = jnp.full((TILE, LANES), by_bit(3, bit))
             total = rate_on + rate_off
             fading = jnp.exp(-total)
             factor_ref[bit] = (rate_off + rate_on * fading) / total
@@ -119,8 +114,8 @@
     def update(buf, slot, row, out=False):
         level = (first + row).astype(jnp.float32)
         side = (total_rows + 3.0 * level) * (1.0 / (4.0 * total_rows))
-        drop = decay_ref[0] * level * (1.0 / total_rows)
-        drop_next = decay_ref[0] * (level + 1.0) * (1.0 / total_rows)
+        drop = decays[0] * level * (1.0 / total_rows)
+        drop_next = decays[0] * (level + 1.0) * (1.0 / total_rows)
         fall, curve = fall_ref[...], curve_ref[...]
         stay = (1.0 - drop) - fall
         values = []
@@ -158,33 +153,36 @@
     def mine(q, row):
         return main.at[slot_of(row)] if q == 0 else arrived[q - 1].at[row]
 
-    def exchange(q, row):
+    forward = list(range(stages))
+    backward = forward[::-1]
+
+    def exchange(q, row, way):
         return pltpu.make_async_remote_copy(
             src_ref=mine(q, row), dst_ref=arrived[q].at[row],
             send_sem=send_sem.at[q, row], recv_sem=recv_sem.at[q, row],
-            device_id=(partners[q], place), device_id_type=MESH)
+            device_id=(partners[way[q]], place), device_id_type=MESH)
 
     def factor(kind, bit):
         return factor_ref[kind * GENES + bit]
 
-    def mix(q, row):
-        bit = local_bits + q
-        on = (gene >> q) & 1 == 1
+    def mix(q, row, way):
+        bit = local_bits + way[q]
+        on = (gene >> way[q]) & 1 == 1
         keep = wide(jnp.where(on, factor(3, bit), factor(0, bit)))
         take = wide(jnp.where(on, factor(2, bit), factor(1, bit)))
         own = mine(q, row)
         return [keep * own[part(i), :] + take * arrived[q][row, part(i), :] for i in range(tiles)]
 
-    def advance(q, row):
-        exchange(q, row).wait_recv()
-        for i, value in enumerate(mix(q, row)):
+    def advance(q, row, way):
+        exchange(q, row, way).wait_recv()
+        for i, value in enumerate(mix(q, row, way)):
             arrived[q][row, part(i), :] = value
-        exchange(q + 1, row).start()
-
-    def finish(row):
+        exchange(q + 1, row, way).start()
+
+    def finish(row, way):
         q = stages - 1
-        exchange(q, row).wait_recv()
-        blocks = mix(q, row)
+        exchange(q, row, way).wait_recv()
+        blocks = mix(q, row, way)
         index = lax.broadcasted_iota(jnp.int32, (TILE, LANES), 0)
         for bit in range(3):
             on = (index >> bit) & 1 == 1
@@ -222,11 +220,12 @@
             device_id=(gene, place - 1), device_id_type=MESH)
         return upward, downward
 
-    def halo_start(copies):
+    def start_up(copies):
         @pl.when(has_next)
         def _():
             copies[0].start()
 
+    def start_down(copies):
         @pl.when(has_prev)
         def _():
             copies[1].start()
@@ -262,92 +261,97 @@
     prepare()
     for block in fetch_order[:2]:
         fetch(block).wait()
-    loop(0, SUB, load_both)
-    loop(rows - SUB, rows, load_main)
+    loop(0, 2 * SUB, load_both)
     met = stages + jnp.where(has_prev, 1, 0) + jnp.where(has_next, 1, 0)
     pl.semaphore_wait(barrier, met)
-
     early_halo = halo(main, edge, halo_send, halo_recv)
-    halo_start(early_halo)
-    loop(SUB, 2 * SUB, load_both)
-    for block in fetch_order[2:]:
-        fetch(block).wait()
+    start_down(early_halo)
     triangle(main, 2 * SUB, 0, SUB - 1)
 
-    def produce(k):
+    def produce(k, way):
         @pl.when(k + 2 < rows - SUB)
         def _():
             load_main(k + 2)
         wave(main, k)
-        exchange(0, k - 2).start()
-
-    def produce_and_pass(k):
-        produce(k)
-        advance(0, k - 3)
+        exchange(0, k - 2, way).start()
 
     early = SUB + EARLY
-    produce(6)
-    loop(7, early + 3, produce_and_pass)
-    loop(early + 3, rows - SUB, produce)
+    produce(6, backward)
+    fetch(fetch_order[2]).wait()
+    loop(rows - SUB, rows, load_main)
+    start_up(early_halo)
+    for block in fetch_order[3:]:
+        fetch(block).wait()
+    loop(7, early + 2, lambda k: produce(k, backward))
+    loop(early + 2, rows - SUB, lambda k: produce(k, forward))
     halo_bottom(early_halo, main)
-    loop(rows - SUB, rows + 2, produce)
+    loop(rows - SUB, rows + 2, lambda k: produce(k, forward))
     halo_top(early_halo, edge)
     triangle(edge, 3 * SUB, -SUB, SUB)
 
     def give(row):
         main[rows - SUB + row] = edge[row]
-        exchange(0, row).start()
+        exchange(0, row, forward).start()
 
     loop(0, SUB, give)
-    order = [(SUB, early), (rows - SUB, rows), (0, SUB), (early, rows - SUB)]
-    for low, high in order[1:]:
-        loop(low, high, lambda row: advance(0, row))
-    for q in range(1, stages - 1):
-        for low, high in order:
-            loop(low, high, lambda row, q=q: advance(q, row))
-
-    for low, high in order[:-1]:
-        loop(low, high, finish)
+    order = [
+        (rows - SUB, rows, forward), (0, SUB, forward), (early, rows - SUB, forward),
+        (SUB, early, backward),
+    ]
+    for q in range(stages - 1):
+        for low, high, way in order:
+            loop(low, high, lambda row, q=q, way=way: advance(q, row, way))
+
+    for low, high, way in order[3:] + order[:2]:
+        loop(low, high, lambda row, way=way: finish(row, way))
 
     def copy_edge(row):
         late_edge[SUB + row] = late[row]
 
     loop(0, 2 * SUB, copy_edge)
     late_halo = halo(late, late_edge, late_send, late_recv)
-    halo_start(late_halo)
+    start_down(late_halo)
+    start_up(late_halo)
 
     def emit(k):
         wave(late, k, out=True)
 
     def finish_and_emit(k):
-        finish(k + 2)
+        finish(k + 2, forward)
         emit(k)
 
     triangle(late, 2 * SUB, 0, SUB - 1)
     loop(6, early - 2, emit)
     loop(early - 2, rows - SUB - 6, finish_and_emit)
-    deliver(1).start()
     halo_top(late_halo, late_edge)
     triangle(late_edge, 3 * SUB, -SUB, SUB - 1)
     loop(0, SUB, lambda j: update(late_edge, j, j, out=True))
-    deliver(0).start()
     loop(rows - SUB - 6, rows - SUB - 2, finish_and_emit)
-    deliver(2).start()
     halo_bottom(late_halo, late)
     loop(rows - SUB - 2, rows + 2, emit)
-    deliver(3).start()
     for q in range(stages):
-        loop(0, rows, lambda row, q=q: exchange(q, row).wait_send())
-    for block in range(blocks_in):
-        deliver(block).wait()
-
-
-def body(peers, genes, density, *params):
+        for low, high, way in order:
+            loop(low, high, lambda row, q=q, way=way: exchange(q, row, way).wait_send())
+
+
+def body(
+    peers, genes, density, effect_first, effect_second, decay_pair, switch_rates, gene_place,
+    bound_first, bound_second,
+):
     count, rows, width = density.shape
+    pieces = [
+        effect_first[None], effect_second[None], switch_rates, gene_place[None], decay_pair[None],
+        bound_first[None], bound_second[None]]
+    sums = {np.float32: 0.0, np.int32: 0}
+    line = 0
+    for piece in pieces:
+        after = TILE - line - piece.shape[0]
+        kind = piece.dtype.type
+        sums[kind] += jnp.pad(piece, ((line, after), (0, LANES - piece.shape[1])))
+        line += piece.shape[0]
+    params = sums[np.float32] + sums[np.int32].astype(jnp.float32)
     stages = genes.bit_length() - 1
     row = (count, width)
-    smem = pl.BlockSpec(memory_space=pltpu.SMEM)
-    whole = pl.BlockSpec(memory_space=pl.ANY)
 
     def vmem(*shape):
         return pltpu.VMEM(shape, jnp.float32)
@@ -355,10 +359,10 @@
     return pl.pallas_call(
         functools.partial(kernel, count, rows, width, peers, float(rows * peers)),
         out_shape=jax.ShapeDtypeStruct(density.shape, jnp.float32),
-        in_specs=[whole] + [smem] * len(params),
-        out_specs=whole,
+        in_specs=[
+            pl.BlockSpec(memory_space=pl.ANY), pl.BlockSpec(memory_space=pltpu.SMEM)],
+        out_specs=pl.BlockSpec(memory_space=pltpu.VMEM),
         scratch_shapes=[
-            vmem(*density.shape),
             vmem(*density.shape),
             vmem(count, LANES),
             vmem(count, LANES),
@@ -379,11 +383,10 @@
             pltpu.SemaphoreType.DMA((2,)),
             pltpu.SemaphoreType.DMA((2,)),
             pltpu.SemaphoreType.DMA((rows // TILE,)),
-            pltpu.SemaphoreType.DMA((rows // TILE,)),
         ],
         compiler_params=pltpu.CompilerParams(
-            collective_id=0, has_side_effects=True, vmem_limit_bytes=60 * 1024 * 1024),
-    )(density, *params)
+            collective_id=0, has_side_effects=True, vmem_limit_bytes=48 * 1024 * 1024),
+    )(density, params)
 
 
 def solution(mesh):

time: 112 us -> 109 us (0.973)
  local copies, waits for them, and re-layouts: 4.79 us -> 2.02 us
  Pallas kernels: 106 us -> 104 us
    unnamed x1, local copies, waits for them, and re-layouts: 4.79 us -> 2.02 us
    pallas_call x1, Pallas kernels: 106 us -> 104 us  [body(): pl.pallas_call(functools.partial(kernel, count, rows, width, peers, float...]
where the time goes in v1:
time: 109 us; the launch traced here: 107 us
  Pallas kernels  104 us (95%)
  local copies, waits for them, and re-layouts  2.02 us (2%)
    pallas_call x1, Pallas kernels, body(): pl.pallas_call(functools.partial(kernel, count, rows, width, peers, float...  104 us

profile of v1, /device:TPU:8, one launch (start us, length us, event | category | flops | bytes accessed | tf_op | source)
XLA Modules:
  0.0 107.1 jit_solution(10305083146590232304)
XLA Ops:
  0.0 0.8 convert_add_fusion.param_ref
  0.8 104.3 %shard_map.82 = f32[32,32,1024]{2,1,0:T(8,128)S(1)} custom-call(f32[32,32,1024]{2,1,0:T(8,128)} %density_ref.1, f32[8,128]{1,0:T(8,128)S(1)} %convert_add_fusion.param_ref), custom_call_target="tpu_custom_call" | custom-call | tf_op jit(solution)/shard_map/pallas_call | solution.py:359
  105.1 2.0 %copy.10 = f32[32,32,1024]{2,1,0:T(8,128)} copy(f32[32,32,1024]{2,1,0:T(8,128)S(1)} %shard_map.82) | data formatting | bytes 8388608

commit v2 on v1

--- a/solution.py
+++ b/solution.py
@@ -12,7 +12,7 @@
 SUB = 4
 TILE = 8
 LANES = 128
-EARLY = 10
+EARLY = 11
 MESH = pl.DeviceIdType.MESH
 
 
@@ -20,7 +20,7 @@
     count, rows, width, peers, total_rows,
     density_ref, param_ref, out_ref,
     x_ref, birth_ref, bound_ref, limit_ref, grow_ref, curve_ref, fall_ref, factor_ref,
-    main, edge, late, late_edge, *rest,
+    main, edge, late, late_edge, foot, *rest,
 ):
     stages = len(rest) - 7
     arrived = rest[:stages]
@@ -98,6 +98,8 @@
             birth_ref[part(i), :] = one
             grow_ref[part(i), :] = jnp.where(
                 cols + 1.0 < wide(limit_ref[part(i), :]), wide(two), 0.0)
+
+    def prepare_factors():
         for bit in range(GENES):
             rate_on = jnp.full((TILE, LANES), by_bit(2, bit))
             rate_off = jnp.full((TILE, LANES), by_bit(3, bit))
@@ -111,7 +113,7 @@
     def load(row):
         return x_ref[:, row, :]
 
-    def update(buf, slot, row, out=False):
+    def update(buf, slot, row, out=False, to=None):
         level = (first + row).astype(jnp.float32)
         side = (total_rows + 3.0 * level) * (1.0 / (4.0 * total_rows))
         drop = decays[0] * level * (1.0 / total_rows)
@@ -135,6 +137,8 @@
         for i, value in enumerate(values):
             if out:
                 out_ref[part(i), row, :] = value
+            elif to is not None:
+                foot[to, part(i), :] = value
             else:
                 buf[slot, part(i), :] = value
 
@@ -277,6 +281,7 @@
 
     early = SUB + EARLY
     produce(6, backward)
+    prepare_factors()
     fetch(fetch_order[2]).wait()
     loop(rows - SUB, rows, load_main)
     start_up(early_halo)
@@ -286,6 +291,7 @@
     loop(early + 2, rows - SUB, lambda k: produce(k, forward))
     halo_bottom(early_halo, main)
     loop(rows - SUB, rows + 2, lambda k: produce(k, forward))
+    loop(rows - SUB, rows, lambda row: advance(0, row, forward))
     halo_top(early_halo, edge)
     triangle(edge, 3 * SUB, -SUB, SUB)
 
@@ -299,7 +305,7 @@
         (SUB, early, backward),
     ]
     for q in range(stages - 1):
-        for low, high, way in order:
+        for low, high, way in order[1 if q == 0 else 0:]:
             loop(low, high, lambda row, q=q, way=way: advance(q, row, way))
 
     for low, high, way in order[3:] + order[:2]:
@@ -326,9 +332,22 @@
     halo_top(late_halo, late_edge)
     triangle(late_edge, 3 * SUB, -SUB, SUB - 1)
     loop(0, SUB, lambda j: update(late_edge, j, j, out=True))
-    loop(rows - SUB - 6, rows - SUB - 2, finish_and_emit)
+    last = rows - SUB - 1
+    loop(rows - SUB - 6, last - 2, finish_and_emit)
     halo_bottom(late_halo, late)
-    loop(rows - SUB - 2, rows + 2, emit)
+    starts = [0, 6, 10, 12]
+    loop(0, 6, lambda j: update(late, last + 1 + j, last + 2 + j, to=j))
+    for t in range(2, SUB):
+        begin, end = starts[t - 1], starts[t]
+        before = starts[t - 2]
+        loop(0, end - begin, lambda j, t=t, begin=begin, before=before: update(
+            foot, before + j, last + 1 + t + j, to=begin + j))
+    finish(last, forward)
+    for t in range(1, SUB + 1):
+        loop(last - t, last + t + 1, lambda row, t=t: update(late, row - t, row, out=t == SUB))
+        if t < SUB:
+            for i in range(2):
+                late[last + 1 + i] = foot[starts[t - 1] + i]
     for q in range(stages):
         for low, high, way in order:
             loop(low, high, lambda row, q=q, way=way: exchange(q, row, way).wait_send())
@@ -375,6 +394,7 @@
             vmem(3 * SUB, *row),
             vmem(rows + SUB, *row),
             vmem(3 * SUB, *row),
+            vmem(3 * SUB, *row),
         ] + [vmem(rows, *row)] * stages + [
             pltpu.SemaphoreType.DMA((stages, rows)),
             pltpu.SemaphoreType.DMA((stages, rows)),

time: 109 us -> 107 us (0.982)
    pallas_call x1, Pallas kernels: 104 us -> 103 us  [body(): pl.pallas_call(functools.partial(kernel, count, rows, width, peers, float...]
where the time goes in v2:
time: 107 us; the launch traced here: 106 us
  Pallas kernels  103 us (96%)
  local copies, waits for them, and re-layouts  2.02 us (2%)
    pallas_call x1, Pallas kernels, body(): pl.pallas_call(functools.partial(kernel, count, rows, width, peers, float...  103 us

profile of v2, /device:TPU:8, one launch (start us, length us, event | category | flops | bytes accessed | tf_op | source)
XLA Modules:
  0.0 105.6 jit_solution(13355498428321809717)
XLA Ops:
  0.0 0.8 convert_add_fusion.param_ref
  0.8 102.8 %shard_map.82 = f32[32,32,1024]{2,1,0:T(8,128)S(1)} custom-call(f32[32,32,1024]{2,1,0:T(8,128)} %density_ref.1, f32[8,128]{1,0:T(8,128)S(1)} %convert_add_fusion.param_ref), custom_call_target="tpu_custom_call" | custom-call | tf_op jit(solution)/shard_map/pallas_call | solution.py:378
  103.6 2.0 %copy.10 = f32[32,32,1024]{2,1,0:T(8,128)} copy(f32[32,32,1024]{2,1,0:T(8,128)S(1)} %shard_map.82) | data formatting | bytes 8388608

commit v3 on v2

--- a/solution.py
+++ b/solution.py
@@ -342,6 +342,10 @@
         before = starts[t - 2]
         loop(0, end - begin, lambda j, t=t, begin=begin, before=before: update(
             foot, before + j, last + 1 + t + j, to=begin + j))
+    for q in range(stages):
+        for low, high, way in order:
+            high = high - SUB if high == last + 1 else high
+            loop(low, high, lambda row, q=q, way=way: exchange(q, row, way).wait_send())
     finish(last, forward)
     for t in range(1, SUB + 1):
         loop(last - t, last + t + 1, lambda row, t=t: update(late, row - t, row, out=t == SUB))
@@ -349,8 +353,7 @@
             for i in range(2):
                 late[last + 1 + i] = foot[starts[t - 1] + i]
     for q in range(stages):
-        for low, high, way in order:
-            loop(low, high, lambda row, q=q, way=way: exchange(q, row, way).wait_send())
+        loop(last - SUB + 1, last + 1, lambda row, q=q: exchange(q, row, forward).wait_send())
 
 
 def body(

time: 107 us -> 107 us (level)
  no operation moved by 1% of the time
where the time goes in v3:
time: 107 us; the launch traced here: 106 us
  Pallas kernels  103 us (96%)
  local copies, waits for them, and re-layouts  2.02 us (2%)
    pallas_call x1, Pallas kernels, body(): pl.pallas_call(functools.partial(kernel, count, rows, width, peers, float...  103 us

profile of v3, /device:TPU:8, one launch (start us, length us, event | category | flops | bytes accessed | tf_op | source)
XLA Modules:
  0.0 105.6 jit_solution(965428828183488130)
XLA Ops:
  0.0 0.8 convert_add_fusion.param_ref
  0.8 102.8 %shard_map.82 = f32[32,32,1024]{2,1,0:T(8,128)S(1)} custom-call(f32[32,32,1024]{2,1,0:T(8,128)} %density_ref.1, f32[8,128]{1,0:T(8,128)S(1)} %convert_add_fusion.param_ref), custom_call_target="tpu_custom_call" | custom-call | tf_op jit(solution)/shard_map/pallas_call | solution.py:381
  103.5 2.0 %copy.10 = f32[32,32,1024]{2,1,0:T(8,128)} copy(f32[32,32,1024]{2,1,0:T(8,128)S(1)} %shard_map.82) | data formatting | bytes 8388608
